TPU v7x, 32 devices: a whole 2x2x4 slice. The times are simulated.
32 devices in a mesh: dp: 8 (over y, x, core), mp: 4 (over z).
Axes of the slice: x: 2, y: 2, z: 4, core: 2. Of those that a mesh axis runs over, the one named last changes fastest.
Arguments:
- query_rows: bfloat16 [2048, 5120], P('dp', 'mp'), may hold values from -160 to 160
- key_rows: bfloat16 [2048, 1024], P('dp', 'mp'), may hold values from -8 to 8
- value_rows: bfloat16 [2048, 1024], P('dp', 'mp'), may hold values from -6 to 6
- grad_out: bfloat16 [2048, 5120], P('dp', 'mp'), may hold values from -6 to 6
- out_proj: bfloat16 [5120, 5120], P('mp'), may hold values from -0.078125 to 0.078125
- lengths: int32 [32, 4], replicated, may hold values from 1 to 48, 64 in all within a row
- offsets: int32 [4], replicated, may hold values from 0 to 7, as said below
Outputs:
- grad_query: bfloat16 [2048, 5120], P('dp', 'mp')
- grad_key: bfloat16 [2048, 1024], P('dp', 'mp')
- grad_value: bfloat16 [2048, 1024], P('dp', 'mp')
- grad_proj: float32 [5120, 5120], P('dp', 'mp')
Inputs may be any that keep to these rules, and one draw needn't show every extreme that they name: Each row is the document lengths of one block, summing to 64; the longest is exactly 48. `offsets`: the 4 values are distinct.
All inputs are finite; a program needn't handle non-finite values.
Results may differ from a plain program's by a relative error of at most 0.033.
Values may be sent and summed in bfloat16 or wider, within the bound.
A program may use at most 128 MiB of HBM per device.

v0:
```python
import jax
import jax.numpy as jnp
from jax import lax
from jax.sharding import PartitionSpec as P

HEADS = 40
KVH = 8
HD = 128


def doc_layout(lengths, block_len):
    doc_ends = jnp.cumsum(lengths, axis=1)
    positions = jnp.arange(block_len, dtype=jnp.int32)
    segment = jnp.sum((doc_ends[:, None, :] <= positions[None, :, None]).astype(jnp.int32), axis=2)
    doc_ids = jnp.arange(lengths.shape[1], dtype=jnp.int32)
    onehot_doc = segment[:, :, None] == doc_ids[None, None, :]
    own_length = jnp.sum(jnp.where(onehot_doc, lengths[:, None, :], 0), axis=2)
    token_weight = 1.0 / own_length.astype(jnp.float32)
    return (segment, token_weight)


def block_grads(query_blk, key_blk, value_blk, grad_blk, segment):
    length = query_blk.shape[0]
    scaling = query_blk.shape[-1] ** (-0.5)
    positions = jnp.arange(length, dtype=jnp.int32)
    allowed = (segment[:, None] == segment[None, :]) & (positions[None, :] <= positions[:, None])
    scores = (
        jnp.einsum("qkgd,pkd->kgqp", query_blk, key_blk, preferred_element_type=jnp.float32)
        * scaling
    )
    scores = jnp.where(allowed[None, None], scores, -1e30)
    top_score = jnp.max(scores, axis=-1, keepdims=True)
    exponent = jnp.where(allowed[None, None], jnp.exp(scores - top_score), 0.0)
    denominator = jnp.sum(exponent, axis=-1, keepdims=True)
    soft = exponent / denominator
    soft_weight = soft.astype(jnp.bfloat16)
    attended = jnp.einsum(
        "kgqp,pkd->qkgd", soft_weight, value_blk, preferred_element_type=jnp.float32
    ).astype(jnp.bfloat16)
    row_dot = jnp.sum(grad_blk.astype(jnp.float32) * attended.astype(jnp.float32), axis=-1)
    grad_soft = jnp.einsum(
        "qkgd,pkd->kgqp", grad_blk, value_blk, preferred_element_type=jnp.float32
    )
    grad_score = (soft * (grad_soft - jnp.transpose(row_dot, (1, 2, 0))[..., None])).astype(
        jnp.bfloat16
    )
    grad_q = (
        jnp.einsum("kgqp,pkd->qkgd", grad_score, key_blk, preferred_element_type=jnp.float32)
        * scaling
    ).astype(jnp.bfloat16)
    grad_k = (
        jnp.einsum("kgqp,qkgd->pkd", grad_score, query_blk, preferred_element_type=jnp.float32)
        * scaling
    ).astype(jnp.bfloat16)
    grad_v = jnp.einsum(
        "kgqp,qkgd->pkd", soft_weight, grad_blk, preferred_element_type=jnp.float32
    ).astype(jnp.bfloat16)
    return (attended, grad_q, grad_k, grad_v)


def local(query_rows, key_rows, value_rows, grad_out, out_proj, lengths, offsets):
    data_ranks = lax.axis_size("dp")
    my_rank = lax.axis_index("dp")
    slot_count = offsets.shape[0]
    block_len = query_rows.shape[0] // slot_count
    slot_ids = jnp.arange(slot_count, dtype=jnp.int32)
    peer_ids = jnp.arange(data_ranks, dtype=jnp.int32)
    targets = (my_rank + offsets) % data_ranks
    sources = (my_rank - offsets) % data_ranks
    home_ids = my_rank * slot_count + slot_ids
    moved_ids = sources * slot_count + slot_ids
    home_segment, home_weight = doc_layout(lengths[home_ids], block_len)
    moved_segment, moved_weight = doc_layout(lengths[moved_ids], block_len)
    weighted = (grad_out.astype(jnp.float32) * home_weight.reshape(-1, 1)).astype(jnp.bfloat16)
    group = HEADS // KVH

    def to_peers(matrix, goal_rank):
        pieces = matrix.reshape(slot_count, block_len, matrix.shape[1])
        matches = goal_rank[None, :] == peer_ids[:, None]
        picked = jnp.sum(jnp.where(matches, slot_ids[None, :], 0), axis=1)
        filled = jnp.any(matches, axis=1)
        return jnp.where(filled[:, None, None], pieces[picked], jnp.zeros((), matrix.dtype))

    def from_peers(tiles, anchor):
        return tiles[anchor].reshape(slot_count * block_len, tiles.shape[2])

    arrived = (
        lax.all_to_all(
            to_peers(query_rows, targets), "dp", split_axis=0, concat_axis=0, tiled=True
        ),
        lax.all_to_all(to_peers(key_rows, targets), "dp", split_axis=0, concat_axis=0, tiled=True),
        lax.all_to_all(
            to_peers(value_rows, targets), "dp", split_axis=0, concat_axis=0, tiled=True
        ),
        lax.all_to_all(to_peers(weighted, targets), "dp", split_axis=0, concat_axis=0, tiled=True),
    )
    whole_cot = lax.all_gather(from_peers(arrived[3], sources), "mp", axis=1, tiled=True)
    head_grad = lax.dot_general(
        whole_cot, out_proj, (((1,), (1,)), ((), ())), preferred_element_type=jnp.float32
    ).astype(jnp.bfloat16)
    query_in = from_peers(arrived[0], sources)
    key_in = from_peers(arrived[1], sources)
    kv_local = key_in.shape[1] // HD
    tokens_here = query_in.shape[0]
    query_blk = query_in.reshape(slot_count, block_len, kv_local, group, HD)
    key_blk = key_in.reshape(slot_count, block_len, kv_local, HD)
    value_blk = from_peers(arrived[2], sources).reshape(slot_count, block_len, kv_local, HD)
    grad_blk = head_grad.reshape(slot_count, block_len, kv_local, group, HD)
    attended, grad_q, grad_k, grad_v = jax.vmap(block_grads)(
        query_blk, key_blk, value_blk, grad_blk, moved_segment
    )
    attended_rows = attended.reshape(tokens_here, query_in.shape[1])
    grad_proj = lax.psum_scatter(
        lax.dot_general(
            whole_cot, attended_rows, (((0,), (0,)), ((), ())), preferred_element_type=jnp.float32
        ),
        "dp",
        scatter_dimension=0,
        tiled=True,
    )
    return (
        grad_q.reshape(tokens_here, query_in.shape[1]),
        grad_k.reshape(tokens_here, key_in.shape[1]),
        grad_v.reshape(tokens_here, key_in.shape[1]),
        grad_proj,
    )


def solution(mesh):
    return jax.shard_map(
        local,
        mesh=mesh,
        in_specs=(
            P("dp", "mp"),
            P("dp", "mp"),
            P("dp", "mp"),
            P("dp", "mp"),
            P("mp", None),
            P(),
            P(),
        ),
        out_specs=(P("dp", "mp"), P("dp", "mp"), P("dp", "mp"), P("dp", "mp")),
        check_vma=False,
    )
```

profile of v0, /device:TPU:0, one launch (start us, length us, event | category | flops | bytes accessed | tf_op | source)
XLA Modules:
  0.0 287.2 jit_solution(2023178399918019281)
XLA Ops:
  7.2 0.7 compare_select_fusion.1
  8.1 0.8 copy.35
  8.9 0.6 gather_fusion.7
  9.9 1.3 multiply_convert_fusion
  11.2 0.6 gather_fusion.8
  11.8 0.6 gather_fusion.3
  12.5 1.8 broadcast_select_fusion
  14.2 5.2 %all-to-all-start.3 = ((bf16[8,64,1280]{2,1,0:T(8,128)(2,1)}), bf16[8,64,1280]{2,1,0:T(8,128)(2,1)S(1)}, u32[]{:S(2)}, u32[]{:S(2)}) async-start(bf16[8,64,1280]{2,1,0:T(8,128)(2,1)} %get-tuple-element.6), calls=%async_computation.3 | async-start | bytes 2621440 | tf_op jit(solution)/shard_map/all_to_all | solution.py:95
  19.5 18.1 %all-to-all-done.3 = bf16[8,64,1280]{2,1,0:T(8,128)(2,1)S(1)} async-done(((bf16[8,64,1280]{2,1,0:T(8,128)(2,1)}), bf16[8,64,1280]{2,1,0:T(8,128)(2,1)S(1)}, u32[]{:S(2)}, u32[]{:S(2)}) %all-to-all-start.3) | async-done | bytes 1310752 | tf_op jit(solution)/shard_map/all_to_all | solution.py:95
  37.6 1.4 gather_fusion.9
  39.1 0.6 gather_fusion.5
  39.7 0.6 gather_fusion
  40.3 9.3 %all_to_all.20 = bf16[8,64,256]{2,1,0:T(8,128)(2,1)S(1)} all-to-all(bf16[8,64,256]{2,1,0:T(8,128)(2,1)S(1)} %get-tuple-element.8), channel_id=1, replica_groups=mesh['dp'=8,'mp'=4] {'dp'}, dimensions={0} | all-to-all | bytes 524288 | tf_op jit(solution)/shard_map/all_to_all | solution.py:91
  49.7 9.3 %all_to_all.21 = bf16[8,64,256]{2,1,0:T(8,128)(2,1)S(1)} all-to-all(bf16[8,64,256]{2,1,0:T(8,128)(2,1)S(1)} %get-tuple-element.9), channel_id=1, replica_groups=mesh['dp'=8,'mp'=4] {'dp'}, dimensions={0} | all-to-all | bytes 524288 | tf_op jit(solution)/shard_map/all_to_all | solution.py:92
  59.0 3.6 %all-to-all-start.1 = ((bf16[8,64,1280]{2,1,0:T(8,128)(2,1)}), bf16[8,64,1280]{2,1,0:T(8,128)(2,1)S(1)}, u32[]{:S(2)}, u32[]{:S(2)}) async-start(bf16[8,64,1280]{2,1,0:T(8,128)(2,1)} %get-tuple-element.7), calls=%async_computation.1 | async-start | bytes 2621440 | tf_op jit(solution)/shard_map/all_to_all | solution.py:88
  62.7 0.6 gather_fusion.2
  64.8 15.9 %all-to-all-done.1 = bf16[8,64,1280]{2,1,0:T(8,128)(2,1)S(1)} async-done(((bf16[8,64,1280]{2,1,0:T(8,128)(2,1)}), bf16[8,64,1280]{2,1,0:T(8,128)(2,1)S(1)}, u32[]{:S(2)}, u32[]{:S(2)}) %all-to-all-start.1) | async-done | bytes 1310752 | tf_op jit(solution)/shard_map/all_to_all | solution.py:88
  80.7 0.6 gather_fusion.4
  81.3 0.7 reshape_reshape.10
  82.1 1.8 fusion.44
  83.9 9.5 %all-gather.2.cloned.1.call-done = bf16[256,5120]{1,0:T(8,128)(2,1)} async-done(((bf16[256,1280]{1,0:T(8,128)(2,1)}), bf16[256,5120]{1,0:T(8,128)(2,1)}) %all-gather.2.cloned.1.call-update) | async-done | bytes 2621456 | tf_op jit(solution)/shard_map/all_gather | solution.py:97
  93.4 9.1 %convolution_convert_fusion = bf16[256,1280]{1,0:T(8,128)(2,1)S(1)} fusion(bf16[256,5120]{1,0:T(8,128)(2,1)} %all-gather.2.cloned.1.call-done, bf16[1280,5120]{1,0:T(8,128)(2,1)} %param.11), kind=kOutput, calls=%fused_computation.11 | convolution fusion | flops 3355770880 | bytes 16384000 | tf_op jit(solution)/shard_map/dot_general | solution.py:98
  102.5 0.7 reshape.111
  103.8 1.2 multiply_reduce_fusion
  105.1 1.4 copy.51
  106.5 1.9 reshape.115
  108.4 10.6 %fusion.49 = f32[5120,1280]{1,0:T(8,128)} fusion(bf16[256,5120]{1,0:T(8,128)(2,1)S(1)} %copy-done.2, bf16[256,1280]{1,0:T(8,128)(2,1)S(1)} %reshape.115), kind=kOutput, calls=%fused_computation.86 | convolution fusion | flops 3355443200 | bytes 29491200 | tf_op jit(solution)/shard_map/dot_general | solution.py:114
  119.0 1.2 copy-done.6
  121.4 0.7 fusion.8
  124.0 1.6 reshape.112
  125.5 0.7 copy_bitcast_fusion
  126.3 154.1 %reduce-scatter.2.cloned.1.call-done = f32[640,1280]{1,0:T(8,128)} async-done(((f32[5120,1280]{1,0:T(8,128)}), f32[640,1280]{1,0:T(8,128)}) %reduce-scatter.2.cloned.1.call-update) | async-done | bytes 3276816 | tf_op jit(solution)/shard_map/reduce_scatter | solution.py:113
  (60 shorter events, 6.1 us)
Async XLA Ops:
  7.2 4.7 %copy-start = (bf16[256,1280]{1,0:T(8,128)(2,1)S(1)}, bf16[256,1280]{1,0:T(8,128)(2,1)}, u32[]{:S(2)}) copy-start(bf16[256,1280]{1,0:T(8,128)(2,1)} %param.7) | copy-start | bytes 1966084
  14.2 23.4 %all-to-all-start.3 = ((bf16[8,64,1280]{2,1,0:T(8,128)(2,1)}), bf16[8,64,1280]{2,1,0:T(8,128)(2,1)S(1)}, u32[]{:S(2)}, u32[]{:S(2)}) async-start(bf16[8,64,1280]{2,1,0:T(8,128)(2,1)} %get-tuple-element.6), calls=%async_computation.3 | async-start | bytes 2621440 | tf_op jit(solution)/shard_map/all_to_all | solution.py:95
  19.4 19.7 %copy-start.7 = (bf16[256,256]{1,0:T(8,128)(2,1)S(1)}, bf16[256,256]{1,0:T(8,128)(2,1)}, u32[]{:S(2)}) copy-start(bf16[256,256]{1,0:T(8,128)(2,1)} %param.9) | copy-start | bytes 393220
  19.4 20.2 %copy-start.8 = (bf16[256,256]{1,0:T(8,128)(2,1)S(1)}, bf16[256,256]{1,0:T(8,128)(2,1)}, u32[]{:S(2)}) copy-start(bf16[256,256]{1,0:T(8,128)(2,1)} %param.8) | copy-start | bytes 393220
  19.4 74.0 %all-gather.2.cloned.1.call-start = ((), (), s32[]{:S(2)}) async-start(), calls=%async_computation.5 | async-start | bytes 3276800 | tf_op jit(solution)/shard_map/all_gather | solution.py:97
  59.0 21.7 %all-to-all-start.1 = ((bf16[8,64,1280]{2,1,0:T(8,128)(2,1)}), bf16[8,64,1280]{2,1,0:T(8,128)(2,1)S(1)}, u32[]{:S(2)}, u32[]{:S(2)}) async-start(bf16[8,64,1280]{2,1,0:T(8,128)(2,1)} %get-tuple-element.7), calls=%async_computation.1 | async-start | bytes 2621440 | tf_op jit(solution)/shard_map/all_to_all | solution.py:88
  62.6 217.8 %reduce-scatter.2.cloned.1.call-start = ((), (), s32[]{:S(2)}) async-start(), calls=%async_computation.6 | async-start | bytes 29491200 | tf_op jit(solution)/shard_map/reduce_scatter | solution.py:113
  82.1 1.9 copy-start.3
  83.9 19.3 %copy-start.12 = (f32[4,2,5,64]{3,2,1,0:T(8,128)}, f32[4,2,5,64]{3,2,1,0:T(8,128)S(1)}, u32[]{:S(2)}) copy-start(f32[4,2,5,64]{3,2,1,0:T(8,128)S(1)} %get-tuple-element.11) | copy-start | bytes 30724
  102.5 1.3 copy-start.10
  103.2 1.8 copy-start.5
  105.1 3.3 %copy-start.2 = (bf16[256,5120]{1,0:T(8,128)(2,1)S(1)}, bf16[256,5120]{1,0:T(8,128)(2,1)}, u32[]{:S(2)}) copy-start(bf16[256,5120]{1,0:T(8,128)(2,1)} %all-gather.2.cloned.1.call-done) | copy-start | bytes 7864324
  119.0 1.2 copy-start.6
  119.0 1.6 copy-start.11
  119.0 1.6 copy-start.13
  120.6 0.8 copy-start.9
  121.4 1.2 copy-start.4
  123.5 156.9 %copy-start.1 = (bf16[256,1280]{1,0:T(8,128)(2,1)S(1)}, bf16[256,1280]{1,0:T(8,128)(2,1)}, u32[]{:S(2)}) copy-start(bf16[256,1280]{1,0:T(8,128)(2,1)} %param.7) | copy-start | bytes 1966084
Sparse Core Ops, SparseCore 0:
  39.2 54.1 all-gather.1
  119.1 161.1 reduce-scatter.1
where the time goes:
time: 288 us; the launch traced here: 287 us
  waiting for transfers between devices  198 us (69%)
  matrix products  24.5 us (9%)
  blocking collectives  18.7 us (6%)
  local copies, waits for them, and re-layouts  18.3 us (6%)
  between operations  14.4 us (5%)
  starting transfers between devices  8.82 us (3%)
  other arithmetic  4.82 us (2%)
    reduce_scatter x1, waiting for transfers between devices, local(): lax.psum_scatter(lax.dot_general(whole_cot, attended_rows, (((0,), (0,)),...  154 us
    all_to_all x1, waiting for transfers between devices, local(): lax.all_to_all(to_peers(weighted, targets), 'dp', split_axis=0, concat_ax...  18.1 us
    all_to_all x1, waiting for transfers between devices, local(): lax.all_to_all(to_peers(query_rows, targets), 'dp', split_axis=0, concat_...  15.9 us
    dot_general x1, matrix products, local(): lax.dot_general(whole_cot, attended_rows, (((0,), (0,)), ((), ())), prefe...  10.6 us
    all_gather x1, waiting for transfers between devices, local(): lax.all_gather(from_peers(arrived[3], sources), 'mp', axis=1, tiled=True)  9.46 us
    all_to_all x1, blocking collectives, local(): lax.all_to_all(to_peers(key_rows, targets), 'dp', split_axis=0, concat_ax...  9.35 us
    all_to_all x1, blocking collectives, local(): lax.all_to_all(to_peers(value_rows, targets), 'dp', split_axis=0, concat_...  9.33 us
    dot_general x1, matrix products, local(): lax.dot_general(whole_cot, out_proj, (((1,), (1,)), ((), ())), preferred_...  9.1 us
  transfers between devices with their start and end apart: 4, of which 4 were waited for; matrix products, arithmetic and copies ran while one was open for 4% of the time, Pallas kernels for 0%

commit v1 on v0

--- a/solution.py
+++ b/solution.py
@@ -62,66 +62,63 @@
     data_ranks = lax.axis_size("dp")
     my_rank = lax.axis_index("dp")
     slot_count = offsets.shape[0]
-    block_len = query_rows.shape[0] // slot_count
+    tokens_here = query_rows.shape[0]
+    block_len = tokens_here // slot_count
     slot_ids = jnp.arange(slot_count, dtype=jnp.int32)
     peer_ids = jnp.arange(data_ranks, dtype=jnp.int32)
     targets = (my_rank + offsets) % data_ranks
     sources = (my_rank - offsets) % data_ranks
-    home_ids = my_rank * slot_count + slot_ids
-    moved_ids = sources * slot_count + slot_ids
-    home_segment, home_weight = doc_layout(lengths[home_ids], block_len)
-    moved_segment, moved_weight = doc_layout(lengths[moved_ids], block_len)
-    weighted = (grad_out.astype(jnp.float32) * home_weight.reshape(-1, 1)).astype(jnp.bfloat16)
+    home_lengths = lax.dynamic_slice_in_dim(lengths, my_rank * slot_count, slot_count, 0)
+    segment, weight = doc_layout(home_lengths, block_len)
+    weighted = (grad_out.astype(jnp.float32) * weight.reshape(-1, 1)).astype(jnp.bfloat16)
     group = HEADS // KVH
+    features = query_rows.shape[1]
+    kv_local = key_rows.shape[1] // HD
 
-    def to_peers(matrix, goal_rank):
-        pieces = matrix.reshape(slot_count, block_len, matrix.shape[1])
-        matches = goal_rank[None, :] == peer_ids[:, None]
-        picked = jnp.sum(jnp.where(matches, slot_ids[None, :], 0), axis=1)
-        filled = jnp.any(matches, axis=1)
-        return jnp.where(filled[:, None, None], pieces[picked], jnp.zeros((), matrix.dtype))
-
-    def from_peers(tiles, anchor):
-        return tiles[anchor].reshape(slot_count * block_len, tiles.shape[2])
-
-    arrived = (
-        lax.all_to_all(
-            to_peers(query_rows, targets), "dp", split_axis=0, concat_axis=0, tiled=True
-        ),
-        lax.all_to_all(to_peers(key_rows, targets), "dp", split_axis=0, concat_axis=0, tiled=True),
-        lax.all_to_all(
-            to_peers(value_rows, targets), "dp", split_axis=0, concat_axis=0, tiled=True
-        ),
-        lax.all_to_all(to_peers(weighted, targets), "dp", split_axis=0, concat_axis=0, tiled=True),
-    )
-    whole_cot = lax.all_gather(from_peers(arrived[3], sources), "mp", axis=1, tiled=True)
+    whole_cot = lax.all_gather(weighted, "mp", axis=1, tiled=True)
+    width = whole_cot.shape[1]
+    gather = data_ranks * tokens_here * (features + width // data_ranks) < width * features
+    if gather:
+        cot_cols = lax.all_to_all(whole_cot, "dp", split_axis=1, concat_axis=0, tiled=True)
     head_grad = lax.dot_general(
         whole_cot, out_proj, (((1,), (1,)), ((), ())), preferred_element_type=jnp.float32
     ).astype(jnp.bfloat16)
-    query_in = from_peers(arrived[0], sources)
-    key_in = from_peers(arrived[1], sources)
-    kv_local = key_in.shape[1] // HD
-    tokens_here = query_in.shape[0]
-    query_blk = query_in.reshape(slot_count, block_len, kv_local, group, HD)
-    key_blk = key_in.reshape(slot_count, block_len, kv_local, HD)
-    value_blk = from_peers(arrived[2], sources).reshape(slot_count, block_len, kv_local, HD)
-    grad_blk = head_grad.reshape(slot_count, block_len, kv_local, group, HD)
     attended, grad_q, grad_k, grad_v = jax.vmap(block_grads)(
-        query_blk, key_blk, value_blk, grad_blk, moved_segment
+        query_rows.reshape(slot_count, block_len, kv_local, group, HD),
+        key_rows.reshape(slot_count, block_len, kv_local, HD),
+        value_rows.reshape(slot_count, block_len, kv_local, HD),
+        head_grad.reshape(slot_count, block_len, kv_local, group, HD),
+        segment,
     )
-    attended_rows = attended.reshape(tokens_here, query_in.shape[1])
-    grad_proj = lax.psum_scatter(
-        lax.dot_general(
-            whole_cot, attended_rows, (((0,), (0,)), ((), ())), preferred_element_type=jnp.float32
-        ),
-        "dp",
-        scatter_dimension=0,
-        tiled=True,
+    attended_rows = attended.reshape(tokens_here, features)
+    if gather:
+        everyone = lax.all_gather(attended_rows, "dp", axis=0, tiled=True)
+        grad_proj = lax.dot_general(
+            cot_cols, everyone, (((0,), (0,)), ((), ())), preferred_element_type=jnp.float32
+        )
+    else:
+        grad_proj = lax.psum_scatter(
+            lax.dot_general(
+                whole_cot, attended_rows, (((0,), (0,)), ((), ())), preferred_element_type=jnp.float32
+            ),
+            "dp",
+            scatter_dimension=0,
+            tiled=True,
+        )
+
+    grads = jnp.concatenate(
+        [part.reshape(slot_count, block_len, -1) for part in (grad_q, grad_k, grad_v)], axis=2
     )
+    matches = targets[None, :] == peer_ids[:, None]
+    picked = jnp.sum(jnp.where(matches, slot_ids[None, :], 0), axis=1)
+    filled = jnp.any(matches, axis=1)
+    parcels = jnp.where(filled[:, None, None], grads[picked], jnp.zeros((), grads.dtype))
+    arrived = lax.all_to_all(parcels, "dp", split_axis=0, concat_axis=0, tiled=True)
+    moved = arrived[sources].reshape(tokens_here, -1)
     return (
-        grad_q.reshape(tokens_here, query_in.shape[1]),
-        grad_k.reshape(tokens_here, key_in.shape[1]),
-        grad_v.reshape(tokens_here, key_in.shape[1]),
+        moved[:, :features],
+        moved[:, features : features + key_rows.shape[1]],
+        moved[:, features + key_rows.shape[1] :],
         grad_proj,
     )
 

time: 288 us -> 180 us (0.62)
  waiting for transfers between devices: 198 us -> 85.4 us
  blocking collectives: 18.7 us -> 31.8 us
  starting transfers between devices: 8.82 us -> 3.89 us
  other arithmetic: 4.82 us -> 1.77 us
    reduce_scatter x1 -> x0, waiting for transfers between devices: 154 us -> none  [local(): lax.psum_scatter(lax.dot_general(whole_cot, attended_rows, (((0,), (0,)),...]
    all_gather x1 -> x2, waiting for transfers between devices: 9.46 us -> 54.5 us  [the longest x1 54.5 us: local(): whole_cot = lax.all_gather(weighted, 'mp', axis=1, tiled=True)]
    all_to_all x2 -> x1, blocking collectives: 18.7 us -> 31.8 us  [local(): lax.all_to_all(parcels, 'dp', split_axis=0, concat_axis=0, tiled=True)]
    all_to_all x2 -> x1, starting transfers between devices: 8.74 us -> 3.81 us  [local(): lax.all_to_all(whole_cot, 'dp', split_axis=1, concat_axis=0, tiled=True)]
    gather x10 -> x2, local copies, waits for them, and re-layouts: 6.63 us -> 2.77 us  [the longest x1 2.11 us: local(): moved = arrived[sources].reshape(tokens_here, -1)]
    all_to_all x2 -> x1, waiting for transfers between devices: 34.1 us -> 30.9 us  [local(): lax.all_to_all(whole_cot, 'dp', split_axis=1, concat_axis=0, tiled=True)]
  transfers between devices with their start and end apart: 4 -> 3, of which waited for: 4 -> 2; matrix products, arithmetic and copies ran while one was open for 4% -> 9% of each run, Pallas kernels for 0% -> 0%
where the time goes in v1:
time: 180 us
  waiting for transfers between devices  85.4 us (47%)
  blocking collectives  31.8 us (18%)
  matrix products  26.4 us (15%)
  local copies, waits for them, and re-layouts  16.1 us (9%)
  between operations  14.3 us (8%)
  starting transfers between devices  3.89 us (2%)
    all_gather x1, waiting for transfers between devices, local(): whole_cot = lax.all_gather(weighted, 'mp', axis=1, tiled=True)  54.5 us
    all_to_all x1, blocking collectives, local(): lax.all_to_all(parcels, 'dp', split_axis=0, concat_axis=0, tiled=True)  31.8 us
    all_to_all x1, waiting for transfers between devices, local(): lax.all_to_all(whole_cot, 'dp', split_axis=1, concat_axis=0, tiled=True)  30.9 us
    dot_general x1, matrix products, local(): lax.dot_general(whole_cot, out_proj, (((1,), (1,)), ((), ())), preferred_...  9.13 us
    dot_general x1, matrix products, local(): lax.dot_general(cot_cols, everyone, (((0,), (0,)), ((), ())), preferred_e...  8.61 us
    unnamed x19, local copies, waits for them, and re-layouts  4.02 us
    all_to_all x1, starting transfers between devices, local(): lax.all_to_all(whole_cot, 'dp', split_axis=1, concat_axis=0, tiled=True)  3.81 us
  transfers between devices with their start and end apart: 3, of which 2 were waited for; matrix products, arithmetic and copies ran while one was open for 9% of the time, Pallas kernels for 0%

profile of v1, /device:TPU:0, one launch (start us, length us, event | category | flops | bytes accessed | tf_op | source)
XLA Modules:
  0.0 179.7 jit_solution(15925431811206496209)
XLA Ops:
  7.2 0.6 copy-done
  8.4 1.3 copy.66
  9.8 1.0 multiply_convert_fusion
  10.9 0.3 copy-done.3
  11.2 0.7 reshape.87
  12.0 0.1 compare_and_fusion
  12.1 1.8 %fusion.44 = (f32[4,2,5,64]{3,2,1,0:T(8,128)S(1)}, f32[4,2,5,64,64]{3,4,2,1,0:T(8,128)}) fusion(pred[4,64,64]{1,2,0:T(8,128)(4,1)S(1)} %compare_and_fusion, bf16[4,64,2,5,128]{4,3,2,1,0:T(8,128)(2,1)S(1)} %reshape.87, bf16[4,64,2,128,1]{3,2,1,0,4:T(2,128)(2,1)S(1)} %bitcast.72), kind=kOutput, calls=%fused_computation.70 | convolution fusion | flops 42762304 | bytes 1468416 | tf_op jit(solution)/shard_map/vmap()/sub | solution.py:33
  13.9 54.5 %all-gather.3.cloned.1.call-done = bf16[256,5120]{0,1:T(8,128)(2,1)} async-done(((bf16[256,1280]{0,1:T(8,128)(2,1)}), bf16[256,5120]{0,1:T(8,128)(2,1)}) %all-gather.3.cloned.1.call-update) | async-done | bytes 2621456 | tf_op jit(solution)/shard_map/all_gather | solution.py:78
  68.5 9.1 %convolution_convert_fusion = bf16[256,1280]{1,0:T(8,128)(2,1)S(1)} fusion(bf16[256,5120]{0,1:T(8,128)(2,1)} %all-gather.3.cloned.1.call-done, bf16[1280,5120]{1,0:T(8,128)(2,1)} %param.11), kind=kOutput, calls=%fused_computation.3 | convolution fusion | flops 3355770880 | bytes 16384000 | tf_op jit(solution)/shard_map/dot_general | solution.py:83
  77.6 0.7 reshape.88
  78.3 2.3 %multiply_reduce_fusion = (f32[4,64,2,5]{1,3,2,0:T(8,128)S(1)}, bf16[4,64,2,5,128]{4,1,3,2,0:T(8,128)(2,1)S(1)}) fusion(bf16[4,64,2,5,128]{4,3,2,1,0:T(8,128)(2,1)S(1)} %reshape.88, bf16[4,64,2,128,1]{3,2,1,0,4:T(2,128)(2,1)S(1)} %bitcast.74, f32[4,2,5,64,64]{3,4,2,1,0:T(8,128)} %get-tuple-element.9, f32[4,2,5,64]{3,2,1,0:T(8,128)S(1)} %get-tuple-element.8), kind=kOutput, calls=%fused_computation.18 | convolution fusion | flops 43906560 | bytes 2117632 | tf_op jit(solution)/shard_map/vmap(kgqp,pkd->qkgd)/dot_general | solution.py:37
  80.7 0.5 copy.82
  81.2 1.6 reshape.94
  83.0 2.0 %fusion.8 = bf16[4,2,5,64,64]{3,4,2,1,0:T(8,128)(2,1)S(1)} fusion(f32[4,2,5,64]{3,2,1,0:T(8,128)S(1)} %bitcast.76, f32[4,2,5,64,64]{3,4,2,1,0:T(8,128)} %get-tuple-element.9, f32[4,2,5,64]{3,2,1,0:T(8,128)S(1)} %get-tuple-element.8, bf16[4,64,2,128,1]{3,2,1,0,4:T(2,128)(2,1)S(1)} %bitcast.75, bf16[4,64,2,5,128]{4,3,2,1,0:T(8,128)(2,1)S(1)} %reshape.88), kind=kOutput, calls=%fused_computation.15 | convolution fusion | flops 42598400 | bytes 1789952 | tf_op jit(solution)/shard_map/vmap(qkgd,pkd->kgqp)/dot_general | solution.py:41
  85.0 0.4 fusion.11
  85.4 0.4 copy-done.4
  85.8 0.5 copy.76
  86.3 0.7 reshape.90
  87.1 0.4 copy-done.5
  87.4 0.3 fusion.16
  87.8 1.0 copy-done.2
  88.7 1.8 fusion.15
  90.6 0.7 gather_fusion
  91.3 0.2 broadcast_select_fusion
  91.5 31.8 %all_to_all.24 = bf16[8,64,1792]{2,1,0:T(8,128)(2,1)} all-to-all(bf16[8,64,1792]{2,1,0:T(8,128)(2,1)S(1)} %broadcast_select_fusion), channel_id=1, replica_groups=mesh['dp'=8,'mp'=4] {'dp'}, dimensions={0} | all-to-all | bytes 3670016 | tf_op jit(solution)/shard_map/all_to_all | solution.py:116
  123.3 3.8 %all-to-all-start.1 = ((bf16[256,8,640]{0,2,1:T(8,128)(2,1)}), bf16[256,8,640]{0,2,1:T(8,128)(2,1)S(1)}, u32[]{:S(2)}, u32[]{:S(2)}) async-start(bf16[256,8,640]{0,2,1:T(8,128)(2,1)} %bitcast.70), calls=%async_computation.1 | async-start | bytes 5242880 | tf_op jit(solution)/shard_map/all_to_all | solution.py:82
  127.1 2.1 %gather_fusion.1 = bf16[4,64,1792]{2,1,0:T(8,128)(2,1)S(1)} fusion(bf16[8,64,1792]{2,1,0:T(8,128)(2,1)} %all_to_all.24, s32[1024]{0:T(1024)S(1)} %pad_clamp_fusion), kind=kCustom, calls=%fused_computation.1 | custom fusion | bytes 1835024 | tf_op jit(solution)/shard_map/gather | solution.py:117
  129.3 0.9 slice.16
  130.1 0.7 fusion.43
  130.9 30.9 %all-to-all-done.1 = bf16[256,8,640]{0,2,1:T(8,128)(2,1)S(1)} async-done(((bf16[256,8,640]{0,2,1:T(8,128)(2,1)}), bf16[256,8,640]{0,2,1:T(8,128)(2,1)S(1)}, u32[]{:S(2)}, u32[]{:S(2)}) %all-to-all-start.1) | async-done | bytes 2621472 | tf_op jit(solution)/shard_map/all_to_all | solution.py:82
  161.7 2.6 %copy.81 = bf16[8,256,640]{2,1,0:T(8,128)(2,1)} copy(bf16[8,256,640]{1,2,0:T(8,128)(2,1)S(1)} %bitcast.67) | data formatting | bytes 5242880 | tf_op jit(solution)/shard_map/all_to_all | solution.py:82
  164.3 8.6 %fusion.49 = f32[640,1280]{1,0:T(8,128)} fusion(bf16[2048,640]{1,0:T(8,128)(2,1)} %bitcast.71, bf16[2048,1280]{1,0:T(8,128)(2,1)} %all-gather.5.cloned.1.call-done), kind=kOutput, calls=%fused_computation.71 | convolution fusion | flops 3355443200 | bytes 11141120 | tf_op jit(solution)/shard_map/dot_general | solution.py:96
  (37 shorter events, 1.1 us)
Async XLA Ops:
  7.2 0.7 copy-start
  7.2 61.3 %all-gather.3.cloned.1.call-start = ((), (), s32[]{:S(2)}) async-start(), calls=%async_computation.2 | async-start | bytes 3276800 | tf_op jit(solution)/shard_map/all_gather | solution.py:78
  9.8 1.1 copy-start.6
  9.8 1.1 copy-start.7
  9.8 1.4 copy-start.3
  10.8 153.5 %all-gather.5.cloned.1.call-start = ((), (), s32[]{:S(2)}) async-start(), calls=%async_computation.3 | async-start | bytes 5898240 | tf_op jit(solution)/shard_map/all_gather | solution.py:95
  78.3 4.7 %copy-start.1 = (bf16[4,64,2,5,128]{4,3,2,1,0:T(8,128)(2,1)}, bf16[4,64,2,5,128]{4,3,2,1,0:T(8,128)(2,1)S(1)}, u32[]{:S(2)}) copy-start(bf16[4,64,2,5,128]{4,3,2,1,0:T(8,128)(2,1)S(1)} %reshape.88) | copy-start | bytes 1966084
  81.2 1.6 copy-start.8
  85.0 0.8 copy-start.4
  86.3 1.1 copy-start.5
  87.4 1.3 copy-start.2
  123.3 38.4 %all-to-all-start.1 = ((bf16[256,8,640]{0,2,1:T(8,128)(2,1)}), bf16[256,8,640]{0,2,1:T(8,128)(2,1)S(1)}, u32[]{:S(2)}, u32[]{:S(2)}) async-start(bf16[256,8,640]{0,2,1:T(8,128)(2,1)} %bitcast.70), calls=%async_computation.1 | async-start | bytes 5242880 | tf_op jit(solution)/shard_map/all_to_all | solution.py:82
Sparse Core Ops, SparseCore 0:
  10.9 57.4 all-gather.2
  82.9 54.6 all-gather.4

commit v2 on v1

--- a/solution.py
+++ b/solution.py
@@ -1,6 +1,10 @@
+import functools
+
 import jax
 import jax.numpy as jnp
 from jax import lax
+from jax.experimental import pallas as pl
+from jax.experimental.pallas import tpu as pltpu
 from jax.sharding import PartitionSpec as P
 
 HEADS = 40
@@ -56,6 +60,222 @@
         "kgqp,qkgd->pkd", soft_weight, grad_blk, preferred_element_type=jnp.float32
     ).astype(jnp.bfloat16)
     return (attended, grad_q, grad_k, grad_v)
+
+
+def push(src, dst, send, recv, **where):
+    return pltpu.make_async_remote_copy(
+        src_ref=src,
+        dst_ref=dst,
+        send_sem=send,
+        recv_sem=recv,
+        device_id=where,
+        device_id_type=pl.DeviceIdType.MESH,
+    )
+
+
+def greet(axis_sizes):
+    barrier = pltpu.get_barrier_semaphore()
+    for axis, size in axis_sizes:
+        for step in range(1, size):
+            pl.semaphore_signal(
+                barrier,
+                inc=1,
+                device_id={axis: (lax.axis_index(axis) + step) % size},
+                device_id_type=pl.DeviceIdType.MESH,
+            )
+    pl.semaphore_wait(barrier, sum(size - 1 for _, size in axis_sizes))
+
+
+CHUNKS = 2
+
+
+def spread_kernel(n_dp, n_mp, own, whole, cols, own_sem, z_send, z_recv, c_send, c_recv, c_own):
+    d, m = lax.axis_index("dp"), lax.axis_index("mp")
+    rows, feat = own.shape
+    piece = cols.shape[2]
+    per = feat // piece
+    part = rows // CHUNKS
+
+    def shard(j, c):
+        return whole.at[pl.ds(c * part, part), pl.ds(pl.multiple_of(j * feat, 128), feat)]
+
+    def hop(way, s, c):
+        j = m - s if way == 0 else m + s
+        src = own.at[pl.ds(c * part, part), :] if s == 0 else shard(j, c)
+        goal = m + 1 if way == 0 else m - 1
+        return push(src, shard(j, c), z_send.at[way, s, c], z_recv.at[way, s, c], mp=goal)
+
+    def sends(way, s):
+        return (m + 1 < n_mp) & (m - s >= 0) if way == 0 else (m >= 1) & (m + s < n_mp)
+
+    def comes(way, s):
+        return m - 1 - s >= 0 if way == 0 else m + 1 + s < n_mp
+
+    def landing(way, s, c):
+        j = m - 1 - s if way == 0 else m + 1 + s
+        came = m - 1 if way == 0 else m + 1
+        return push(shard(j, c), shard(j, c), z_send.at[way, s, c], z_recv.at[way, s, c], mp=came)
+
+    def pass_columns(j, mine):
+        for p in range(per):
+            goal = j * per + p
+            if mine:
+                src = own.at[:, pl.ds(p * piece, piece)]
+            else:
+                src = whole.at[:, pl.ds(pl.multiple_of(j * feat + p * piece, 128), piece)]
+
+            @pl.when(goal == d)
+            def _():
+                pltpu.make_async_copy(src, cols.at[d], c_own).start()
+
+            @pl.when(goal != d)
+            def _():
+                push(src, cols.at[d], c_send.at[goal], c_recv.at[d], dp=goal).start()
+
+    greet((("dp", n_dp), ("mp", n_mp)))
+    for c in range(CHUNKS):
+        for way in range(2):
+
+            @pl.when(sends(way, 0))
+            def _():
+                hop(way, 0, c).start()
+
+    keep = pltpu.make_async_copy(
+        own, whole.at[:, pl.ds(pl.multiple_of(m * feat, 128), feat)], own_sem
+    )
+    keep.start()
+    pass_columns(m, True)
+    for s in range(n_mp - 1):
+        for c in range(CHUNKS):
+            for way in range(2):
+
+                @pl.when(comes(way, s))
+                def _():
+                    landing(way, s, c).wait_recv()
+                    if s + 1 < n_mp - 1:
+
+                        @pl.when(sends(way, s + 1))
+                        def _():
+                            hop(way, s + 1, c).start()
+
+        for way in range(2):
+
+            @pl.when(comes(way, s))
+            def _():
+                pass_columns(m - 1 - s if way == 0 else m + 1 + s, False)
+
+    keep.wait()
+    for s in range(n_mp - 1):
+        for c in range(CHUNKS):
+            for way in range(2):
+
+                @pl.when(sends(way, s))
+                def _():
+                    hop(way, s, c).wait_send()
+
+    sample = own.at[:, pl.ds(0, piece)]
+    pltpu.make_async_copy(sample, cols.at[d], c_own).wait()
+    for peer in range(n_dp):
+
+        @pl.when(peer != d)
+        def _():
+            copy = push(sample, cols.at[peer], c_send.at[peer], c_recv.at[peer], dp=peer)
+            copy.wait_send()
+            copy.wait_recv()
+
+
+def share_kernel(
+    n_dp, own, parcels, everyone, arrived, own_sem, a_send, a_recv, f_send, f_recv, p_send, p_recv
+):
+    d = lax.axis_index("dp")
+    chips = n_dp // 2
+    chip, core = d // 2, d % 2
+    mate = chip * 2 + 1 - core
+    greet((("dp", n_dp),))
+    for k in range(1, chips):
+        goal = ((chip + k) % chips) * 2 + core
+        push(own, everyone.at[d], a_send.at[k], a_recv.at[k], dp=goal).start()
+    push(own, everyone.at[d], a_send.at[0], a_recv.at[0], dp=mate).start()
+    for k in range(1, n_dp):
+        goal = (d + k) % n_dp
+        push(parcels.at[goal], arrived.at[d], p_send.at[k], p_recv.at[k], dp=goal).start()
+    keeps = (
+        pltpu.make_async_copy(own, everyone.at[d], own_sem.at[0]),
+        pltpu.make_async_copy(parcels.at[d], arrived.at[d], own_sem.at[1]),
+    )
+    for keep in keeps:
+        keep.start()
+
+    def passed(k, side, goal):
+        block = everyone.at[((chip + chips - k) % chips) * 2 + side]
+        return push(block, block, f_send.at[k], f_recv.at[k], dp=goal)
+
+    for k in range(1, chips):
+        origin = ((chip + chips - k) % chips) * 2 + core
+        push(own, everyone.at[origin], a_send.at[k], a_recv.at[k], dp=origin).wait_recv()
+        passed(k, core, mate).start()
+    push(own, everyone.at[mate], a_send.at[0], a_recv.at[0], dp=mate).wait_recv()
+    for k in range(1, n_dp):
+        origin = (d + n_dp - k) % n_dp
+        copy = push(parcels.at[d], arrived.at[origin], p_send.at[k], p_recv.at[k], dp=origin)
+        copy.wait_recv()
+        copy.wait_send()
+    for k in range(1, chips):
+        passed(k, 1 - core, mate).wait_recv()
+        passed(k, core, mate).wait_send()
+    for k in range(chips):
+        push(own, everyone.at[d], a_send.at[k], a_recv.at[k], dp=mate).wait_send()
+    for keep in keeps:
+        keep.wait()
+
+
+def spread(weighted, n_dp, n_mp):
+    rows, feat = weighted.shape
+    piece = feat * n_mp // n_dp
+    dma = pltpu.SemaphoreType.DMA
+    anywhere = pl.BlockSpec(memory_space=pl.ANY)
+    return pl.pallas_call(
+        functools.partial(spread_kernel, n_dp, n_mp),
+        out_shape=(
+            jax.ShapeDtypeStruct((rows, feat * n_mp), weighted.dtype),
+            jax.ShapeDtypeStruct((n_dp, rows, piece), weighted.dtype),
+        ),
+        in_specs=[anywhere],
+        out_specs=(anywhere, anywhere),
+        scratch_shapes=[
+            dma(()),
+            dma((2, n_mp - 1, CHUNKS)),
+            dma((2, n_mp - 1, CHUNKS)),
+            dma((n_dp,)),
+            dma((n_dp,)),
+            dma(()),
+        ],
+        compiler_params=pltpu.CompilerParams(collective_id=0, has_side_effects=True),
+    )(weighted)
+
+
+def share(rows, parcels, n_dp):
+    dma = pltpu.SemaphoreType.DMA
+    anywhere = pl.BlockSpec(memory_space=pl.ANY)
+    return pl.pallas_call(
+        functools.partial(share_kernel, n_dp),
+        out_shape=(
+            jax.ShapeDtypeStruct((n_dp, *rows.shape), rows.dtype),
+            jax.ShapeDtypeStruct(parcels.shape, parcels.dtype),
+        ),
+        in_specs=[anywhere, anywhere],
+        out_specs=(anywhere, anywhere),
+        scratch_shapes=[
+            dma((2,)),
+            dma((n_dp // 2,)),
+            dma((n_dp // 2,)),
+            dma((n_dp // 2,)),
+            dma((n_dp // 2,)),
+            dma((n_dp,)),
+            dma((n_dp,)),
+        ],
+        compiler_params=pltpu.CompilerParams(collective_id=1, has_side_effects=True),
+    )(rows, parcels)
 
 
 def local(query_rows, key_rows, value_rows, grad_out, out_proj, lengths, offsets):
@@ -75,11 +295,19 @@
     features = query_rows.shape[1]
     kv_local = key_rows.shape[1] // HD
 
-    whole_cot = lax.all_gather(weighted, "mp", axis=1, tiled=True)
-    width = whole_cot.shape[1]
+    line = lax.axis_size("mp")
+    width = features * line
     gather = data_ranks * tokens_here * (features + width // data_ranks) < width * features
-    if gather:
-        cot_cols = lax.all_to_all(whole_cot, "dp", split_axis=1, concat_axis=0, tiled=True)
+    piece = width // data_ranks
+    fits = width % data_ranks == 0 and piece % 128 == 0 and features % piece == 0
+    kernels = gather and fits and data_ranks % 2 == 0 and block_len % 16 == 0
+    if kernels:
+        whole_cot, cot_cols = spread(weighted, data_ranks, line)
+        cot_cols = cot_cols.reshape(-1, piece)
+    else:
+        whole_cot = lax.all_gather(weighted, "mp", axis=1, tiled=True)
+        if gather:
+            cot_cols = lax.all_to_all(whole_cot, "dp", split_axis=1, concat_axis=0, tiled=True)
     head_grad = lax.dot_general(
         whole_cot, out_proj, (((1,), (1,)), ((), ())), preferred_element_type=jnp.float32
     ).astype(jnp.bfloat16)
@@ -91,8 +319,21 @@
         segment,
     )
     attended_rows = attended.reshape(tokens_here, features)
+    grads = jnp.concatenate(
+        [part.reshape(slot_count, block_len, -1) for part in (grad_q, grad_k, grad_v)], axis=2
+    )
+    matches = targets[None, :] == peer_ids[:, None]
+    picked = jnp.sum(jnp.where(matches, slot_ids[None, :], 0), axis=1)
+    filled = jnp.any(matches, axis=1)
+    parcels = jnp.where(filled[:, None, None], grads[picked], jnp.zeros((), grads.dtype))
+    if kernels:
+        everyone, arrived = share(attended_rows, parcels, data_ranks)
+        everyone = everyone.reshape(-1, features)
+    else:
+        arrived = lax.all_to_all(parcels, "dp", split_axis=0, concat_axis=0, tiled=True)
     if gather:
-        everyone = lax.all_gather(attended_rows, "dp", axis=0, tiled=True)
+        if not kernels:
+            everyone = lax.all_gather(attended_rows, "dp", axis=0, tiled=True)
         grad_proj = lax.dot_general(
             cot_cols, everyone, (((0,), (0,)), ((), ())), preferred_element_type=jnp.float32
         )
@@ -105,15 +346,6 @@
             scatter_dimension=0,
             tiled=True,
         )
-
-    grads = jnp.concatenate(
-        [part.reshape(slot_count, block_len, -1) for part in (grad_q, grad_k, grad_v)], axis=2
-    )
-    matches = targets[None, :] == peer_ids[:, None]
-    picked = jnp.sum(jnp.where(matches, slot_ids[None, :], 0), axis=1)
-    filled = jnp.any(matches, axis=1)
-    parcels = jnp.where(filled[:, None, None], grads[picked], jnp.zeros((), grads.dtype))
-    arrived = lax.all_to_all(parcels, "dp", split_axis=0, concat_axis=0, tiled=True)
     moved = arrived[sources].reshape(tokens_here, -1)
     return (
         moved[:, :features],

time: 180 us -> 170 us (0.944)
  Pallas kernels: 0 us -> 128 us
  waiting for transfers between devices: 85.4 us -> 0 us
  blocking collectives: 31.8 us -> 0 us
  between operations: 14.3 us -> 0.85 us
  local copies, waits for them, and re-layouts: 16.1 us -> 11.2 us
  starting transfers between devices: 3.89 us -> 0 us
  other arithmetic: 1.77 us -> 4.13 us
  matrix products: 26.4 us -> 24.2 us
    pallas_call x0 -> x2, Pallas kernels: none -> 128 us  [the longest x1 64.9 us: share(): pl.pallas_call(functools.partial(share_kernel, n_dp), out_shape=(jax.Shap...]
    all_gather x2 -> x0, waiting for transfers between devices: 54.5 us -> none  [the longest x1 54.5 us: local(): whole_cot = lax.all_gather(weighted, 'mp', axis=1, tiled=True)]
    all_to_all x1 -> x0, blocking collectives: 31.8 us -> none  [local(): lax.all_to_all(parcels, 'dp', split_axis=0, concat_axis=0, tiled=True)]
    all_to_all x1 -> x0, waiting for transfers between devices: 30.9 us -> none  [local(): lax.all_to_all(whole_cot, 'dp', split_axis=1, concat_axis=0, tiled=True)]
    all_to_all x1 -> x0, starting transfers between devices: 3.81 us -> none  [local(): lax.all_to_all(whole_cot, 'dp', split_axis=1, concat_axis=0, tiled=True)]
    all_to_all x1 -> x0, local copies, waits for them, and re-layouts: 2.57 us -> none  [local(): lax.all_to_all(whole_cot, 'dp', split_axis=1, concat_axis=0, tiled=True)]
    unnamed x19 -> x14, local copies, waits for them, and re-layouts: 4.02 us -> 1.51 us
  transfers between devices with their start and end apart: 3 -> 0, of which waited for: 2 -> 0; matrix products, arithmetic and copies ran while one was open for 9% -> 0% of each run, Pallas kernels for 0% -> 0%
where the time goes in v2:
time: 170 us; the launch traced here: 169 us
  Pallas kernels  128 us (75%)
  matrix products  24.2 us (14%)
  local copies, waits for them, and re-layouts  11.2 us (7%)
  other arithmetic  4.13 us (2%)
    pallas_call x1, Pallas kernels, share(): pl.pallas_call(functools.partial(share_kernel, n_dp), out_shape=(jax.Shap...  64.9 us
    pallas_call x1, Pallas kernels, spread(): pl.pallas_call(functools.partial(spread_kernel, n_dp, n_mp), out_shape=(j...  63.6 us
    dot_general x1, matrix products, local(): lax.dot_general(whole_cot, out_proj, (((1,), (1,)), ((), ())), preferred_...  9.1 us
    dot_general x1, matrix products, local(): lax.dot_general(cot_cols, everyone, (((0,), (0,)), ((), ())), preferred_e...  8.09 us

profile of v2, /device:TPU:0, one launch (start us, length us, event | category | flops | bytes accessed | tf_op | source)
XLA Modules:
  0.0 168.8 jit_solution(11237221272103579189)
XLA Ops:
  0.7 0.7 copy-done
  1.4 0.1 copy.49
  1.5 0.1 copy.43
  1.6 0.1 convert_reduce_fusion
  1.7 0.1 select_reduce_fusion
  1.9 2.1 %multiply_convert_fusion.own = bf16[256,1280]{1,0:T(8,128)(2,1)} fusion(bf16[256,1280]{1,0:T(8,128)(2,1)} %param.10, f32[256]{0:T(256)S(1)} %div.25), kind=kLoop, calls=%fused_computation.20 | loop fusion | flops 983040 | bytes 1311744 | tf_op jit(solution)/shard_map/convert_element_type | solution.py:293
  4.0 63.6 %shard_map.102 = (bf16[256,5120]{1,0:T(8,128)(2,1)}, bf16[8,256,640]{2,1,0:T(8,128)(2,1)}) custom-call(bf16[256,1280]{1,0:T(8,128)(2,1)} %multiply_convert_fusion.own), custom_call_target="tpu_custom_call" | custom-call | tf_op jit(solution)/shard_map/pallas_call | solution.py:237
  67.6 9.1 %convolution_convert_fusion = bf16[256,1280]{1,0:T(8,128)(2,1)S(1)} fusion(bf16[256,5120]{1,0:T(8,128)(2,1)} %get-tuple-element.8, bf16[1280,5120]{1,0:T(8,128)(2,1)} %param.11), kind=kOutput, calls=%fused_computation.4 | convolution fusion | flops 3355770880 | bytes 16384000 | tf_op jit(solution)/shard_map/dot_general | solution.py:311
  76.7 0.7 reshape.89
  77.5 0.1 copy-done.2
  77.7 0.1 compare_and_fusion
  77.8 0.1 copy-done.1
  77.9 0.7 reshape.86
  78.7 1.8 %fusion.44 = (f32[4,2,5,64]{3,2,1,0:T(8,128)S(1)}, f32[4,2,5,64,64]{3,4,2,1,0:T(8,128)}) fusion(pred[4,64,64]{1,2,0:T(8,128)(4,1)S(1)} %compare_and_fusion, bf16[4,64,2,5,128]{4,3,2,1,0:T(8,128)(2,1)S(1)} %reshape.86, bf16[4,64,2,128,1]{3,2,1,0,4:T(2,128)(2,1)S(1)} %bitcast.68), kind=kOutput, calls=%fused_computation.71 | convolution fusion | flops 42762304 | bytes 1468416 | tf_op jit(solution)/shard_map/vmap()/sub | solution.py:37
  80.5 2.0 %multiply_reduce_fusion = (f32[4,64,2,5]{1,3,2,0:T(8,128)S(1)}, bf16[4,64,2,5,128]{4,1,3,2,0:T(8,128)(2,1)S(1)}) fusion(bf16[4,64,2,5,128]{4,3,2,1,0:T(8,128)(2,1)S(1)} %reshape.89, bf16[4,64,2,128,1]{3,2,1,0,4:T(2,128)(2,1)S(1)} %bitcast.70, f32[4,2,5,64,64]{3,4,2,1,0:T(8,128)} %get-tuple-element.17, f32[4,2,5,64]{3,2,1,0:T(8,128)S(1)} %get-tuple-element.16), kind=kOutput, calls=%fused_computation.19 | convolution fusion | flops 43906560 | bytes 2117632 | tf_op jit(solution)/shard_map/vmap(kgqp,pkd->qkgd)/dot_general | solution.py:41
  82.5 0.5 copy.48
  82.9 1.6 reshape.88.own
  84.5 1.8 %fusion.15 = bf16[4,2,8,8,128]{4,3,2,1,0:T(8,128)(2,1)S(1)} fusion(bf16[4,64,2,5,128]{4,3,2,1,0:T(8,128)(2,1)S(1)} %reshape.89, f32[4,2,5,64,64]{3,4,2,1,0:T(8,128)} %get-tuple-element.17, f32[4,2,5,64]{3,2,1,0:T(8,128)S(1)} %get-tuple-element.16), kind=kOutput, calls=%fused_computation.28 | convolution fusion | flops 42336256 | bytes 1452032 | tf_op jit(solution)/shard_map/vmap(kgqp,qkgd->pkd)/dot_general | solution.py:59
  86.3 0.7 fusion.8
  87.0 0.3 fusion.16
  87.4 0.4 fusion.11
  87.8 0.5 copy.56
  88.3 0.7 reshape.90
  89.1 0.6 copy-done.4
  89.8 0.7 gather_fusion
  90.5 0.1 fusion.30
  90.5 1.4 broadcast_select_fusion.parcels
  92.0 64.9 %shard_map.103 = (bf16[8,256,1280]{2,1,0:T(8,128)(2,1)}, bf16[8,64,1792]{2,1,0:T(8,128)(2,1)}) custom-call(bf16[256,1280]{1,0:T(8,128)(2,1)} %reshape.88.own, bf16[8,64,1792]{2,1,0:T(8,128)(2,1)} %broadcast_select_fusion.parcels), custom_call_target="tpu_custom_call" | custom-call | tf_op jit(solution)/shard_map/pallas_call | solution.py:260
  156.9 2.3 %gather_fusion.1 = bf16[4,64,1792]{2,1,0:T(8,128)(2,1)S(1)} fusion(bf16[8,64,1792]{2,1,0:T(8,128)(2,1)} %get-tuple-element.9, s32[1024]{0:T(1024)S(1)} %pad_clamp_fusion), kind=kCustom, calls=%fused_computation.1 | custom fusion | bytes 1835024 | tf_op jit(solution)/shard_map/gather | solution.py:349
  159.1 0.9 slice.16
  160.0 0.7 fusion.43
  160.7 8.1 %convolution_bitcast_fusion = f32[640,1280]{1,0:T(8,128)} fusion(bf16[8,256,640]{2,1,0:T(8,128)(2,1)S(1)} %copy-done.5, bf16[8,256,1280]{2,1,0:T(8,128)(2,1)} %get-tuple-element.11), kind=kOutput, calls=%fused_computation.3 | convolution fusion | flops 3355443200 | bytes 11141120 | tf_op jit(solution)/shard_map/dot_general | solution.py:337
  (24 shorter events, 0.5 us)
Async XLA Ops:
  0.6 0.7 copy-start
  76.7 0.9 copy-start.2
  76.7 1.2 copy-start.1
  77.6 1.0 copy-start.3
  84.5 1.8 %copy-start.6 = (f32[4,2,5,64,64]{3,4,2,1,0:T(8,128)S(1)}, f32[4,2,5,64,64]{3,4,2,1,0:T(8,128)}, u32[]{:S(2)}) copy-start(f32[4,2,5,64,64]{3,4,2,1,0:T(8,128)} %get-tuple-element.17) | copy-start | bytes 1966084
  89.0 0.7 copy-start.4
  156.9 3.9 %copy-start.5 = (bf16[8,256,640]{2,1,0:T(8,128)(2,1)S(1)}, bf16[8,256,640]{2,1,0:T(8,128)(2,1)}, u32[]{:S(2)}) copy-start(bf16[8,256,640]{2,1,0:T(8,128)(2,1)} %get-tuple-element.10) | copy-start | bytes 7864324

commit v3 on v2

--- a/solution.py
+++ b/solution.py
@@ -185,15 +185,28 @@
 
 
 def share_kernel(
-    n_dp, own, parcels, everyone, arrived, own_sem, a_send, a_recv, f_send, f_recv, p_send, p_recv
+    n_dp, own, parcels, everyone, arrived, own_sem, a_send, a_recv, f_send, f_recv, p_send, p_recv, r_send, r_recv
 ):
     d = lax.axis_index("dp")
     chips = n_dp // 2
     chip, core = d // 2, d % 2
     mate = chip * 2 + 1 - core
+    square = chips == 4
+    half = own.shape[0] // 2
+
+    def facing(k):
+        if square:
+            other = ((chip // 2) * 2 + 1 - chip % 2, (1 - chip // 2) * 2 + chip % 2, 3 - chip)[k - 1]
+            return other, other
+        return (chip + k) % chips, (chip + chips - k) % chips
+
+    def relay(way, block_of, goal):
+        part = everyone.at[block_of, pl.ds(way * half, half), :]
+        return push(part, part, r_send.at[way], r_recv.at[way], dp=goal)
+
     greet((("dp", n_dp),))
-    for k in range(1, chips):
-        goal = ((chip + k) % chips) * 2 + core
+    for k in range(1, 3 if square else chips):
+        goal = facing(k)[0] * 2 + core
         push(own, everyone.at[d], a_send.at[k], a_recv.at[k], dp=goal).start()
     push(own, everyone.at[d], a_send.at[0], a_recv.at[0], dp=mate).start()
     for k in range(1, n_dp):
@@ -207,12 +220,18 @@
         keep.start()
 
     def passed(k, side, goal):
-        block = everyone.at[((chip + chips - k) % chips) * 2 + side]
+        block = everyone.at[facing(k)[1] * 2 + side]
         return push(block, block, f_send.at[k], f_recv.at[k], dp=goal)
 
     for k in range(1, chips):
-        origin = ((chip + chips - k) % chips) * 2 + core
-        push(own, everyone.at[origin], a_send.at[k], a_recv.at[k], dp=origin).wait_recv()
+        origin = facing(k)[1] * 2 + core
+        if square and k == 3:
+            for way in range(2):
+                relay(way, origin, facing(2 - way)[0] * 2 + core).wait_recv()
+        else:
+            push(own, everyone.at[origin], a_send.at[k], a_recv.at[k], dp=origin).wait_recv()
+            if square:
+                relay(k - 1, origin, facing(3 - k)[0] * 2 + core).start()
         passed(k, core, mate).start()
     push(own, everyone.at[mate], a_send.at[0], a_recv.at[0], dp=mate).wait_recv()
     for k in range(1, n_dp):
@@ -223,8 +242,11 @@
     for k in range(1, chips):
         passed(k, 1 - core, mate).wait_recv()
         passed(k, core, mate).wait_send()
-    for k in range(chips):
+    for k in range(3 if square else chips):
         push(own, everyone.at[d], a_send.at[k], a_recv.at[k], dp=mate).wait_send()
+    if square:
+        for way in range(2):
+            relay(way, facing(way + 1)[1] * 2 + core, mate).wait_send()
     for keep in keeps:
         keep.wait()
 
@@ -273,6 +295,8 @@
             dma((n_dp // 2,)),
             dma((n_dp,)),
             dma((n_dp,)),
+            dma((2,)),
+            dma((2,)),
         ],
         compiler_params=pltpu.CompilerParams(collective_id=1, has_side_effects=True),
     )(rows, parcels)
@@ -300,7 +324,7 @@
     gather = data_ranks * tokens_here * (features + width // data_ranks) < width * features
     piece = width // data_ranks
     fits = width % data_ranks == 0 and piece % 128 == 0 and features % piece == 0
-    kernels = gather and fits and data_ranks % 2 == 0 and block_len % 16 == 0
+    kernels = gather and fits and data_ranks % 2 == 0 and block_len % 16 == 0 and tokens_here % 32 == 0
     if kernels:
         whole_cot, cot_cols = spread(weighted, data_ranks, line)
         cot_cols = cot_cols.reshape(-1, piece)

time: 170 us -> 165 us (0.971)
  Pallas kernels: 128 us -> 125 us
    pallas_call x1, Pallas kernels: 64.9 us -> 61 us  [share(): pl.pallas_call(functools.partial(share_kernel, n_dp), out_shape=(jax.Shap...]
where the time goes in v3:
time: 165 us
  Pallas kernels  125 us (76%)
  matrix products  24.2 us (15%)
  local copies, waits for them, and re-layouts  11.2 us (7%)
  other arithmetic  4.13 us (3%)
    pallas_call x1, Pallas kernels, spread(): pl.pallas_call(functools.partial(spread_kernel, n_dp, n_mp), out_shape=(j...  63.6 us
    pallas_call x1, Pallas kernels, share(): pl.pallas_call(functools.partial(share_kernel, n_dp), out_shape=(jax.Shap...  61 us
    dot_general x1, matrix products, local(): lax.dot_general(whole_cot, out_proj, (((1,), (1,)), ((), ())), preferred_...  9.1 us
    dot_general x1, matrix products, local(): lax.dot_general(cot_cols, everyone, (((0,), (0,)), ((), ())), preferred_e...  8.09 us

profile of v3, /device:TPU:0, one launch (start us, length us, event | category | flops | bytes accessed | tf_op | source)
XLA Modules:
  0.0 164.9 jit_solution(9275190255900149890)
XLA Ops:
  0.7 0.7 copy-done
  1.4 0.1 copy.49
  1.5 0.1 copy.43
  1.6 0.1 convert_reduce_fusion
  1.7 0.1 select_reduce_fusion
  1.9 2.1 %multiply_convert_fusion.own = bf16[256,1280]{1,0:T(8,128)(2,1)} fusion(bf16[256,1280]{1,0:T(8,128)(2,1)} %param.10, f32[256]{0:T(256)S(1)} %div.25), kind=kLoop, calls=%fused_computation.20 | loop fusion | flops 983040 | bytes 1311744 | tf_op jit(solution)/shard_map/convert_element_type | solution.py:317
  4.0 63.6 %shard_map.102 = (bf16[256,5120]{1,0:T(8,128)(2,1)}, bf16[8,256,640]{2,1,0:T(8,128)(2,1)}) custom-call(bf16[256,1280]{1,0:T(8,128)(2,1)} %multiply_convert_fusion.own), custom_call_target="tpu_custom_call" | custom-call | tf_op jit(solution)/shard_map/pallas_call | solution.py:259
  67.6 9.1 %convolution_convert_fusion = bf16[256,1280]{1,0:T(8,128)(2,1)S(1)} fusion(bf16[256,5120]{1,0:T(8,128)(2,1)} %get-tuple-element.8, bf16[1280,5120]{1,0:T(8,128)(2,1)} %param.11), kind=kOutput, calls=%fused_computation.4 | convolution fusion | flops 3355770880 | bytes 16384000 | tf_op jit(solution)/shard_map/dot_general | solution.py:335
  76.7 0.7 reshape.89
  77.5 0.1 copy-done.2
  77.7 0.1 compare_and_fusion
  77.8 0.1 copy-done.1
  77.9 0.7 reshape.86
  78.7 1.8 %fusion.44 = (f32[4,2,5,64]{3,2,1,0:T(8,128)S(1)}, f32[4,2,5,64,64]{3,4,2,1,0:T(8,128)}) fusion(pred[4,64,64]{1,2,0:T(8,128)(4,1)S(1)} %compare_and_fusion, bf16[4,64,2,5,128]{4,3,2,1,0:T(8,128)(2,1)S(1)} %reshape.86, bf16[4,64,2,128,1]{3,2,1,0,4:T(2,128)(2,1)S(1)} %bitcast.68), kind=kOutput, calls=%fused_computation.71 | convolution fusion | flops 42762304 | bytes 1468416 | tf_op jit(solution)/shard_map/vmap()/sub | solution.py:37
  80.5 2.0 %multiply_reduce_fusion = (f32[4,64,2,5]{1,3,2,0:T(8,128)S(1)}, bf16[4,64,2,5,128]{4,1,3,2,0:T(8,128)(2,1)S(1)}) fusion(bf16[4,64,2,5,128]{4,3,2,1,0:T(8,128)(2,1)S(1)} %reshape.89, bf16[4,64,2,128,1]{3,2,1,0,4:T(2,128)(2,1)S(1)} %bitcast.70, f32[4,2,5,64,64]{3,4,2,1,0:T(8,128)} %get-tuple-element.17, f32[4,2,5,64]{3,2,1,0:T(8,128)S(1)} %get-tuple-element.16), kind=kOutput, calls=%fused_computation.19 | convolution fusion | flops 43906560 | bytes 2117632 | tf_op jit(solution)/shard_map/vmap(kgqp,pkd->qkgd)/dot_general | solution.py:41
  82.5 0.5 copy.48
  82.9 1.6 reshape.88.own
  84.5 1.8 %fusion.15 = bf16[4,2,8,8,128]{4,3,2,1,0:T(8,128)(2,1)S(1)} fusion(bf16[4,64,2,5,128]{4,3,2,1,0:T(8,128)(2,1)S(1)} %reshape.89, f32[4,2,5,64,64]{3,4,2,1,0:T(8,128)} %get-tuple-element.17, f32[4,2,5,64]{3,2,1,0:T(8,128)S(1)} %get-tuple-element.16), kind=kOutput, calls=%fused_computation.28 | convolution fusion | flops 42336256 | bytes 1452032 | tf_op jit(solution)/shard_map/vmap(kgqp,qkgd->pkd)/dot_general | solution.py:59
  86.3 0.7 fusion.8
  87.0 0.3 fusion.16
  87.4 0.4 fusion.11
  87.8 0.5 copy.56
  88.3 0.7 reshape.90
  89.1 0.6 copy-done.4
  89.8 0.7 gather_fusion
  90.5 0.1 fusion.30
  90.5 1.4 broadcast_select_fusion.parcels
  92.0 61.0 %shard_map.103 = (bf16[8,256,1280]{2,1,0:T(8,128)(2,1)}, bf16[8,64,1792]{2,1,0:T(8,128)(2,1)}) custom-call(bf16[256,1280]{1,0:T(8,128)(2,1)} %reshape.88.own, bf16[8,64,1792]{2,1,0:T(8,128)(2,1)} %broadcast_select_fusion.parcels), custom_call_target="tpu_custom_call" | custom-call | tf_op jit(solution)/shard_map/pallas_call | solution.py:282
  153.0 2.3 %gather_fusion.1 = bf16[4,64,1792]{2,1,0:T(8,128)(2,1)S(1)} fusion(bf16[8,64,1792]{2,1,0:T(8,128)(2,1)} %get-tuple-element.9, s32[1024]{0:T(1024)S(1)} %pad_clamp_fusion), kind=kCustom, calls=%fused_computation.1 | custom fusion | bytes 1835024 | tf_op jit(solution)/shard_map/gather | solution.py:373
  155.2 0.9 slice.16
  156.1 0.7 fusion.43
  156.8 8.1 %convolution_bitcast_fusion = f32[640,1280]{1,0:T(8,128)} fusion(bf16[8,256,640]{2,1,0:T(8,128)(2,1)S(1)} %copy-done.5, bf16[8,256,1280]{2,1,0:T(8,128)(2,1)} %get-tuple-element.11), kind=kOutput, calls=%fused_computation.3 | convolution fusion | flops 3355443200 | bytes 11141120 | tf_op jit(solution)/shard_map/dot_general | solution.py:361
  (24 shorter events, 0.5 us)
Async XLA Ops:
  0.6 0.7 copy-start
  76.7 0.9 copy-start.2
  76.7 1.2 copy-start.1
  77.6 1.0 copy-start.3
  84.5 1.8 %copy-start.6 = (f32[4,2,5,64,64]{3,4,2,1,0:T(8,128)S(1)}, f32[4,2,5,64,64]{3,4,2,1,0:T(8,128)}, u32[]{:S(2)}) copy-start(f32[4,2,5,64,64]{3,4,2,1,0:T(8,128)} %get-tuple-element.17) | copy-start | bytes 1966084
  89.0 0.7 copy-start.4
  152.9 3.9 %copy-start.5 = (bf16[8,256,640]{2,1,0:T(8,128)(2,1)S(1)}, bf16[8,256,640]{2,1,0:T(8,128)(2,1)}, u32[]{:S(2)}) copy-start(bf16[8,256,640]{2,1,0:T(8,128)(2,1)} %get-tuple-element.10) | copy-start | bytes 7864324
